TPU v7x, 512 devices: a whole 4x8x8 slice. The times are simulated.
512 devices in a mesh: row: 8 (over x, core), col: 16 (over y_lo, z), layer: 4 (over y_hi).
Axes of the slice: x: 4, y: 8 (y_hi: 4, y_lo: 2; y = y_hi * 2 + y_lo), z: 8, core: 2. Of those that a mesh axis runs over, the one named last changes fastest.
Arguments:
- hamiltonian: bfloat16 [8192, 8192], P('row', ('col', 'layer')), as said below
- inv_root: bfloat16 [8192, 8192], P('row', 'col'), as said below
- h_pattern: int32 [32, 32], replicated, may hold values from 0 to 1, as said below
- z_pattern: int32 [32, 32], replicated, may hold values from 0 to 1, as said below
Outputs:
- transformed: bfloat16 [8192, 8192], P('row', ('col', 'layer'))
Inputs may be any that keep to these rules, and one draw needn't show every extreme that they name: hamiltonian is symmetric. inv_root is symmetric. h_pattern is symmetric and every diagonal block is present. z_pattern is symmetric and every diagonal block is present.
All inputs are finite; a program needn't handle non-finite values.
Results may differ from a plain program's by a relative error of at most 0.005.
Values may be sent and summed in bfloat16 or wider, within the bound.
A program may use at most 64 MiB of HBM per device.

v0:
```python
import jax
import jax.numpy as jnp
from jax import lax
from jax.sharding import PartitionSpec as P

BS = 256


def mask_tile(tile, pattern, row_start, col_start):
    blocks = pattern.shape[0]
    block_ids = jnp.arange(blocks, dtype=jnp.int32)
    row_ids = (row_start + jnp.arange(tile.shape[0], dtype=jnp.int32)) // BS
    col_ids = (col_start + jnp.arange(tile.shape[1], dtype=jnp.int32)) // BS
    row_pick = (row_ids[:, None] == block_ids[None, :]).astype(jnp.float32)
    col_pick = (block_ids[:, None] == col_ids[None, :]).astype(jnp.float32)
    inner = jnp.dot(pattern.astype(jnp.float32), col_pick, precision=lax.Precision.HIGHEST)
    keep = jnp.dot(row_pick, inner, precision=lax.Precision.HIGHEST)
    return jnp.where(keep > 0.5, tile, jnp.zeros_like(tile))


def accumulate(left, right):
    return jnp.dot(left, right, preferred_element_type=jnp.float32)


def local(hamiltonian, inv_root, h_pattern, z_pattern):
    rows_here = inv_root.shape[0]
    cols_here = inv_root.shape[1]
    quarter = hamiltonian.shape[1]
    layers = lax.axis_size("layer")
    per_row = lax.axis_size("col") // lax.axis_size("row")
    row_index = lax.axis_index("row")
    col_index = lax.axis_index("col")
    layer_index = lax.axis_index("layer")
    h_local = mask_tile(
        hamiltonian, h_pattern, row_index * rows_here, col_index * cols_here + layer_index * quarter
    )
    z_local = mask_tile(inv_root, z_pattern, row_index * rows_here, col_index * cols_here)
    h_whole = lax.all_gather(h_local, "col", axis=1, tiled=True)
    z_layered = z_local.reshape(per_row, layers, quarter, cols_here)
    z_part = lax.dynamic_index_in_dim(z_layered, layer_index, 1, keepdims=False).reshape(
        per_row * quarter, cols_here
    )
    columns = h_whole
    partial_y = accumulate(columns, lax.all_gather(z_part, "row", axis=0, tiled=True))
    z_quarter = lax.dynamic_slice_in_dim(z_local, layer_index * quarter, quarter, 1)
    z_rows = lax.all_gather(z_quarter, "col", axis=1, tiled=True)
    summed = lax.psum(partial_y, "layer")
    layered = summed.reshape(per_row, layers, quarter, cols_here)
    own_rows = lax.dynamic_index_in_dim(layered, layer_index, 1, keepdims=False).reshape(
        per_row * quarter, cols_here
    )
    y_own = own_rows.astype(jnp.bfloat16)
    columns = z_rows
    partial_c = accumulate(columns, lax.all_gather(y_own, "row", axis=0, tiled=True))
    result = lax.psum_scatter(partial_c, "layer", scatter_dimension=1, tiled=True)
    return result.astype(jnp.bfloat16)


def solution(mesh):
    return jax.shard_map(
        local,
        mesh=mesh,
        in_specs=(P("row", ("col", "layer")), P("row", "col"), P(), P()),
        out_specs=P("row", ("col", "layer")),
        check_vma=False,
    )
```

profile of v0, /device:TPU:20, one launch (start us, length us, event | category | flops | bytes accessed | tf_op | source)
XLA Modules:
  0.0 365.5 jit_solution(18108361089963021768)
XLA Ops:
  6.6 1.1 fusion.4
  7.7 2.3 compare_select_fusion
  10.0 0.7 constant_dynamic-slice_fusion
  10.7 0.0 all-gather.9.cloned.1.call-update
  10.7 0.0 all-gather.7.cloned.1.call-start
  10.8 0.2 fusion.7
  11.1 1.2 fusion
  12.2 0.0 all-gather.7.cloned.1.call-update
  12.3 0.0 all-gather.5.cloned.1.call-start
  12.3 0.7 constant_dynamic-slice_fusion.1
  13.1 0.0 all-gather.5.cloned.1.call-update
  13.1 0.0 all-gather.11.cloned.1.call-start
  13.1 31.7 %all-gather.9.cloned.1.call-done = bf16[2048,512]{1,0:T(8,128)(2,1)} async-done(((bf16[256,512]{1,0:T(8,128)(2,1)}), bf16[2048,512]{1,0:T(8,128)(2,1)}) %all-gather.9.cloned.1.call-update) | async-done | bytes 2097168 | tf_op jit(solution)/shard_map/all_gather | solution.py:44
  44.9 95.0 %all-gather.7.cloned.1.call-done = bf16[1024,2048]{1,0:T(8,128)(2,1)} async-done(((bf16[1024,128]{1,0:T(8,128)(2,1)}), bf16[1024,2048]{1,0:T(8,128)(2,1)}) %all-gather.7.cloned.1.call-update) | async-done | bytes 4194320 | tf_op jit(solution)/shard_map/all_gather | solution.py:38
  139.8 5.2 %fusion.19 = f32[1024,512]{1,0:T(8,128)S(1)} fusion(bf16[1024,2048]{1,0:T(8,128)(2,1)} %all-gather.7.cloned.1.call-done, bf16[2048,512]{1,0:T(8,128)(2,1)} %all-gather.9.cloned.1.call-done), kind=kOutput, calls=%fused_computation.41 | convolution fusion | flops 2147483648 | bytes 8388608 | tf_op jit(solution)/shard_map/dot_general | solution.py:22
  145.0 90.8 %all-reduce.1 = bf16[2,4,128,512]{3,2,1,0:T(8,128)(2,1)S(1)} all-reduce(f32[2,4,128,512]{3,2,1,0:T(8,128)S(1)} %bitcast.10), channel_id=1, replica_groups=mesh['row'=8,'col'=16,'layer'=4] {'layer'}, use_global_device_ids=true, to_apply=%region_0.1 | all-reduce | flops 524288 | bytes 3145728 | tf_op jit(solution)/shard_map/psum | solution.py:47
  235.8 0.7 dynamic-slice_convert_fusion
  236.6 0.0 reduce-scatter.2.cloned.1.call-start
  236.6 30.9 %all-gather.5.cloned.1.call-done = bf16[1024,2048]{1,0:T(8,128)(2,1)} async-done(((bf16[1024,128]{1,0:T(8,128)(2,1)}), bf16[1024,2048]{1,0:T(8,128)(2,1)}) %all-gather.5.cloned.1.call-update) | async-done | bytes 4194320 | tf_op jit(solution)/shard_map/all_gather | solution.py:46
  267.5 28.2 %all-gather.11.cloned.1.call-done = bf16[2048,512]{1,0:T(8,128)(2,1)} async-done(((bf16[256,512]{1,0:T(8,128)(2,1)}), bf16[2048,512]{1,0:T(8,128)(2,1)}) %all-gather.11.cloned.1.call-update) | async-done | bytes 2097168 | tf_op jit(solution)/shard_map/all_gather | solution.py:54
  295.6 6.5 %fusion.20 = f32[1024,512]{1,0:T(8,128)} fusion(bf16[1024,2048]{1,0:T(8,128)(2,1)} %all-gather.5.cloned.1.call-done, bf16[2048,512]{1,0:T(8,128)(2,1)} %all-gather.11.cloned.1.call-done), kind=kOutput, calls=%fused_computation.42 | convolution fusion | flops 2147483648 | bytes 8388608 | tf_op jit(solution)/shard_map/dot_general | solution.py:22
  302.2 0.0 reduce-scatter.2.cloned.1.call-update
  302.2 55.0 %reduce-scatter.2.cloned.1.call-done = f32[1024,128]{1,0:T(8,128)} async-done(((f32[1024,512]{1,0:T(8,128)}), f32[1024,128]{1,0:T(8,128)}) %reduce-scatter.2.cloned.1.call-update) | async-done | bytes 524304 | tf_op jit(solution)/shard_map/reduce_scatter | solution.py:55
  357.2 1.8 convert_element_type.23
  (9 shorter events, 0.1 us)
Async XLA Ops:
  6.5 4.3 %copy-start = (s32[32,32]{1,0:T(8,128)S(1)}, s32[32,32]{1,0:T(8,128)}, u32[]{:S(2)}) copy-start(s32[32,32]{1,0:T(8,128)} %param.6) | copy-start | bytes 12292
  6.5 4.5 %copy-start.1 = (bf16[1024,128]{1,0:T(8,128)(2,1)S(1)}, bf16[1024,128]{1,0:T(8,128)(2,1)}, u32[]{:S(2)}) copy-start(bf16[1024,128]{1,0:T(8,128)(2,1)} %param.4) | copy-start | bytes 786436
  6.5 38.3 %all-gather.9.cloned.1.call-start = ((), (), s32[]{:S(2)}) async-start(), calls=%async_computation.3 | async-start | bytes 2359296 | tf_op jit(solution)/shard_map/all_gather | solution.py:44
  10.7 129.1 %all-gather.7.cloned.1.call-start = ((), (), s32[]{:S(2)}) async-start(), calls=%async_computation.2 | async-start | bytes 4456448 | tf_op jit(solution)/shard_map/all_gather | solution.py:38
  12.3 255.2 %all-gather.5.cloned.1.call-start = ((), (), s32[]{:S(2)}) async-start(), calls=%async_computation.1 | async-start | bytes 4456448 | tf_op jit(solution)/shard_map/all_gather | solution.py:46
  13.1 282.6 %all-gather.11.cloned.1.call-start = ((), (), s32[]{:S(2)}) async-start(), calls=%async_computation.4 | async-start | bytes 2359296 | tf_op jit(solution)/shard_map/all_gather | solution.py:54
  236.6 120.7 %reduce-scatter.2.cloned.1.call-start = ((), (), s32[]{:S(2)}) async-start(), calls=%async_computation.5 | async-start | bytes 2621440 | tf_op jit(solution)/shard_map/reduce_scatter | solution.py:55
Sparse Core Ops, SparseCore 0:
  10.9 33.9 all-gather.8
  46.9 92.9 all-gather.6
  141.9 125.5 all-gather.4
  269.5 26.1 all-gather.10
  302.3 54.8 reduce-scatter.1
where the time goes:
time: 366 us
  waiting for transfers between devices  241 us (66%)
  blocking collectives  90.8 us (25%)
  matrix products  16.5 us (5%)
  between operations  13.2 us (4%)
    all_gather x1, waiting for transfers between devices, local(): h_whole = lax.all_gather(h_local, 'col', axis=1, tiled=True)  95 us
    psum x1, blocking collectives, local(): summed = lax.psum(partial_y, 'layer')  90.8 us
    reduce_scatter x1, waiting for transfers between devices, local(): lax.psum_scatter(partial_c, 'layer', scatter_dimension=1, tiled=True)  55 us
    all_gather x1, waiting for transfers between devices, local(): lax.all_gather(z_part, 'row', axis=0, tiled=True)  31.7 us
    all_gather x1, waiting for transfers between devices, local(): z_rows = lax.all_gather(z_quarter, 'col', axis=1, tiled=True)  30.9 us
    all_gather x1, waiting for transfers between devices, local(): lax.all_gather(y_own, 'row', axis=0, tiled=True)  28.2 us
    dot_general x2, matrix products, accumulate(): return jnp.dot(left, right, preferred_element_type=jnp.float32)  11.7 us
  transfers between devices with their start and end apart: 5, of which 5 were waited for; matrix products, arithmetic and copies ran while one was open for 2% of the time, Pallas kernels for 0%

commit v1 on v0

--- a/solution.py
+++ b/solution.py
@@ -4,6 +4,19 @@
 from jax.sharding import PartitionSpec as P
 
 BS = 256
+
+
+def ring_gather(x, axis, dim):
+    ways = lax.axis_size(axis)
+    up = [(d, (d + 1) % ways) for d in range(ways)]
+    down = [(d, (d - 1) % ways) for d in range(ways)]
+    earlier, later = ([x], [x])
+    for _ in range(ways // 2):
+        earlier.append(lax.ppermute(earlier[-1], axis, up))
+    for _ in range((ways - 1) // 2):
+        later.append(lax.ppermute(later[-1], axis, down))
+    line = jnp.concatenate([*earlier[::-1], *later[1:]], axis=dim)
+    return jnp.roll(line, (lax.axis_index(axis) - ways // 2) * x.shape[dim], axis=dim)
 
 
 def mask_tile(tile, pattern, row_start, col_start):
@@ -41,7 +54,7 @@
         per_row * quarter, cols_here
     )
     columns = h_whole
-    partial_y = accumulate(columns, lax.all_gather(z_part, "row", axis=0, tiled=True))
+    partial_y = accumulate(columns, ring_gather(z_part, "row", 0))
     z_quarter = lax.dynamic_slice_in_dim(z_local, layer_index * quarter, quarter, 1)
     z_rows = lax.all_gather(z_quarter, "col", axis=1, tiled=True)
     summed = lax.psum(partial_y, "layer")

time: 366 us -> 334 us (0.913)
  waiting for transfers between devices: 241 us -> 191 us
  local copies, waits for them, and re-layouts: 2.21 us -> 13.1 us
  starting transfers between devices: 0.17 us -> 5.78 us
    all_gather x1, waiting for transfers between devices: 95 us -> 57.1 us  [local(): h_whole = lax.all_gather(h_local, 'col', axis=1, tiled=True)]
    all_gather x1 -> x0, waiting for transfers between devices: 31.7 us -> none  [local(): lax.all_gather(z_part, 'row', axis=0, tiled=True)]
    ppermute x0 -> x7, waiting for transfers between devices: none -> 17.5 us  [the longest x4 17.5 us: ring_gather(): earlier.append(lax.ppermute(earlier[-1], axis, up))]
    unnamed x4 -> x15, local copies, waits for them, and re-layouts: 0.01 us -> 10.9 us
    ppermute x0 -> x7, starting transfers between devices: none -> 5.65 us  [the longest x3 5.63 us: ring_gather(): later.append(lax.ppermute(later[-1], axis, down))]
  transfers between devices with their start and end apart: 5 -> 11, of which waited for: 5 -> 8; matrix products, arithmetic and copies ran while one was open for 2% -> 6% of each run, Pallas kernels for 0% -> 0%
where the time goes in v1:
time: 334 us; the launch traced here: 333 us
  waiting for transfers between devices  191 us (57%)
  blocking collectives  90.5 us (27%)
  matrix products  18.1 us (5%)
  between operations  13.2 us (4%)
  local copies, waits for them, and re-layouts  13.1 us (4%)
  starting transfers between devices  5.78 us (2%)
    psum x1, blocking collectives, local(): summed = lax.psum(partial_y, 'layer')  90.5 us
    all_gather x1, waiting for transfers between devices, local(): h_whole = lax.all_gather(h_local, 'col', axis=1, tiled=True)  57.1 us
    reduce_scatter x1, waiting for transfers between devices, local(): lax.psum_scatter(partial_c, 'layer', scatter_dimension=1, tiled=True)  55 us
    all_gather x1, waiting for transfers between devices, local(): z_rows = lax.all_gather(z_quarter, 'col', axis=1, tiled=True)  31.3 us
    all_gather x1, waiting for transfers between devices, local(): lax.all_gather(y_own, 'row', axis=0, tiled=True)  29.8 us
    ppermute x4, waiting for transfers between devices, ring_gather(): earlier.append(lax.ppermute(earlier[-1], axis, up))  17.5 us
    dot_general x2, matrix products, accumulate(): return jnp.dot(left, right, preferred_element_type=jnp.float32)  11.7 us
    unnamed x15, local copies, waits for them, and re-layouts  10.9 us
  transfers between devices with their start and end apart: 11, of which 8 were waited for; matrix products, arithmetic and copies ran while one was open for 6% of the time, Pallas kernels for 0%

profile of v1, /device:TPU:20, one launch (start us, length us, event | category | flops | bytes accessed | tf_op | source)
XLA Modules:
  0.0 333.3 jit_solution(18170141652305973481)
XLA Ops:
  6.6 1.0 fusion.9
  7.5 2.1 fusion.2
  9.8 1.0 fusion.6
  10.8 2.3 compare_select_fusion
  13.1 0.7 constant_dynamic-slice_fusion.1
  14.0 5.8 %collective-permute-done = bf16[256,512]{1,0:T(8,128)(2,1)S(1)} collective-permute-done((bf16[256,512]{1,0:T(8,128)(2,1)S(1)}, bf16[256,512]{1,0:T(8,128)(2,1)S(1)}, u32[]{:S(2)}, u32[]{:S(2)}) %collective-permute-start) | collective-permute-done | bytes 262176 | tf_op jit(solution)/shard_map/ppermute | solution.py:15
  19.8 1.7 collective-permute-start.4
  21.5 4.1 %collective-permute-done.1 = bf16[256,512]{1,0:T(8,128)(2,1)S(1)} collective-permute-done((bf16[256,512]{1,0:T(8,128)(2,1)S(1)}, bf16[256,512]{1,0:T(8,128)(2,1)S(1)}, u32[]{:S(2)}, u32[]{:S(2)}) %collective-permute-start.1) | collective-permute-done | bytes 262176 | tf_op jit(solution)/shard_map/ppermute | solution.py:15
  25.6 1.7 collective-permute-start.5
  27.3 4.0 %collective-permute-done.2 = bf16[256,512]{1,0:T(8,128)(2,1)S(1)} collective-permute-done((bf16[256,512]{1,0:T(8,128)(2,1)S(1)}, bf16[256,512]{1,0:T(8,128)(2,1)S(1)}, u32[]{:S(2)}, u32[]{:S(2)}) %collective-permute-start.2) | collective-permute-done | bytes 262176 | tf_op jit(solution)/shard_map/ppermute | solution.py:15
  31.4 2.1 collective-permute-start.6
  33.5 3.6 %collective-permute-done.3 = bf16[256,512]{1,0:T(8,128)(2,1)S(1)} collective-permute-done((bf16[256,512]{1,0:T(8,128)(2,1)S(1)}, bf16[256,512]{1,0:T(8,128)(2,1)S(1)}, u32[]{:S(2)}, u32[]{:S(2)}) %collective-permute-start.3) | collective-permute-done | bytes 262176 | tf_op jit(solution)/shard_map/ppermute | solution.py:15
  37.2 0.7 constant_dynamic-update-slice_fusion.15
  37.9 0.7 constant_dynamic-update-slice_fusion.14
  38.7 0.7 constant_dynamic-update-slice_fusion.13
  39.4 0.7 constant_dynamic-update-slice_fusion.12
  48.8 57.1 %all-gather.6.cloned.1.call-done = bf16[1024,2048]{1,0:T(8,128)(2,1)} async-done(((bf16[1024,128]{1,0:T(8,128)(2,1)}), bf16[1024,2048]{1,0:T(8,128)(2,1)}) %all-gather.6.cloned.1.call-update) | async-done | bytes 4194320 | tf_op jit(solution)/shard_map/all_gather | solution.py:51
  105.9 5.2 %fusion = f32[1024,512]{1,0:T(8,128)S(1)} fusion(bf16[1024,2048]{1,0:T(8,128)(2,1)} %all-gather.6.cloned.1.call-done, bf16[4096,512]{1,0:T(8,128)(2,1)} %constant_dynamic-update-slice_fusion, s32[]{:T(128)S(6)} %select_n.66), kind=kOutput, calls=%fused_computation | convolution fusion | flops 2147483648 | bytes 8388612 | tf_op jit(solution)/shard_map/dot_general | solution.py:35
  111.1 90.5 %all-reduce.1 = bf16[2,4,128,512]{3,2,1,0:T(8,128)(2,1)S(1)} all-reduce(f32[2,4,128,512]{3,2,1,0:T(8,128)S(1)} %bitcast.13), channel_id=1, replica_groups=mesh['row'=8,'col'=16,'layer'=4] {'layer'}, use_global_device_ids=true, to_apply=%region_0.1 | all-reduce | flops 524288 | bytes 3145728 | tf_op jit(solution)/shard_map/psum | solution.py:60
  202.4 31.3 %all-gather.4.cloned.1.call-done = bf16[1024,2048]{1,0:T(8,128)(2,1)} async-done(((bf16[1024,128]{1,0:T(8,128)(2,1)}), bf16[1024,2048]{1,0:T(8,128)(2,1)}) %all-gather.4.cloned.1.call-update) | async-done | bytes 4194320 | tf_op jit(solution)/shard_map/all_gather | solution.py:59
  233.7 29.8 %all-gather.8.cloned.1.call-done = bf16[2048,512]{1,0:T(8,128)(2,1)} async-done(((bf16[256,512]{1,0:T(8,128)(2,1)}), bf16[2048,512]{1,0:T(8,128)(2,1)}) %all-gather.8.cloned.1.call-update) | async-done | bytes 2097168 | tf_op jit(solution)/shard_map/all_gather | solution.py:67
  263.4 6.5 %fusion.22 = f32[1024,512]{1,0:T(8,128)} fusion(bf16[1024,2048]{1,0:T(8,128)(2,1)} %all-gather.4.cloned.1.call-done, bf16[2048,512]{1,0:T(8,128)(2,1)} %all-gather.8.cloned.1.call-done), kind=kOutput, calls=%fused_computation.60 | convolution fusion | flops 2147483648 | bytes 8388608 | tf_op jit(solution)/shard_map/dot_general | solution.py:35
  270.0 55.0 %reduce-scatter.2.cloned.1.call-done = f32[1024,128]{1,0:T(8,128)} async-done(((f32[1024,512]{1,0:T(8,128)}), f32[1024,128]{1,0:T(8,128)}) %reduce-scatter.2.cloned.1.call-update) | async-done | bytes 524304 | tf_op jit(solution)/shard_map/reduce_scatter | solution.py:68
  325.0 1.8 convert_element_type.23
  (32 shorter events, 9.7 us)
Async XLA Ops:
  6.5 99.4 %all-gather.6.cloned.1.call-start = ((), (), s32[]{:S(2)}) async-start(), calls=%async_computation.2 | async-start | bytes 4456448 | tf_op jit(solution)/shard_map/all_gather | solution.py:51
  9.7 224.0 %all-gather.4.cloned.1.call-start = ((), (), s32[]{:S(2)}) async-start(), calls=%async_computation.1 | async-start | bytes 4456448 | tf_op jit(solution)/shard_map/all_gather | solution.py:59
  13.9 249.5 %all-gather.8.cloned.1.call-start = ((), (), s32[]{:S(2)}) async-start(), calls=%async_computation.3 | async-start | bytes 2359296 | tf_op jit(solution)/shard_map/all_gather | solution.py:67
  14.0 5.8 %collective-permute-start = (bf16[256,512]{1,0:T(8,128)(2,1)S(1)}, bf16[256,512]{1,0:T(8,128)(2,1)S(1)}, u32[]{:S(2)}, u32[]{:S(2)}) collective-permute-start(bf16[256,512]{1,0:T(8,128)(2,1)S(1)} %bitcast.9), channel_id=1, source_target_pairs={{0,64},{64,128},{128,192},{192,256},{256,320},{320,384},{384,448},... | collective-permute-start | bytes 786440 | tf_op jit(solution)/shard_map/ppermute | solution.py:15
  19.8 5.8 %collective-permute-start.1 = (bf16[256,512]{1,0:T(8,128)(2,1)S(1)}, bf16[256,512]{1,0:T(8,128)(2,1)S(1)}, u32[]{:S(2)}, u32[]{:S(2)}) collective-permute-start(bf16[256,512]{1,0:T(8,128)(2,1)S(1)} %collective-permute-done), channel_id=1, source_target_pairs={{0,64},{64,128},{128,192},{192,256},{256,320},{320,384},{384,448},... | collective-permute-start | bytes 786440 | tf_op jit(solution)/shard_map/ppermute | solution.py:15
  19.8 5.8 %collective-permute-start.4 = (bf16[256,512]{1,0:T(8,128)(2,1)S(1)}, bf16[256,512]{1,0:T(8,128)(2,1)S(1)}, u32[]{:S(2)}, u32[]{:S(2)}) collective-permute-start(bf16[256,512]{1,0:T(8,128)(2,1)S(1)} %bitcast.10), channel_id=1, source_target_pairs={{0,448},{64,0},{128,64},{192,128},{256,192},{320,256},{384,320},{4... | collective-permute-start | bytes 786440 | tf_op jit(solution)/shard_map/ppermute | solution.py:17
  25.6 5.8 %collective-permute-start.2 = (bf16[256,512]{1,0:T(8,128)(2,1)S(1)}, bf16[256,512]{1,0:T(8,128)(2,1)S(1)}, u32[]{:S(2)}, u32[]{:S(2)}) collective-permute-start(bf16[256,512]{1,0:T(8,128)(2,1)S(1)} %collective-permute-done.1), channel_id=1, source_target_pairs={{0,64},{64,128},{128,192},{192,256},{256,320},{320,384},{384,448},... | collective-permute-start | bytes 786440 | tf_op jit(solution)/shard_map/ppermute | solution.py:15
  25.6 5.8 %collective-permute-start.5 = (bf16[256,512]{1,0:T(8,128)(2,1)S(1)}, bf16[256,512]{1,0:T(8,128)(2,1)S(1)}, u32[]{:S(2)}, u32[]{:S(2)}) collective-permute-start(bf16[256,512]{1,0:T(8,128)(2,1)S(1)} %collective-permute-done.4), channel_id=1, source_target_pairs={{0,448},{64,0},{128,64},{192,128},{256,192},{320,256},{384,320},{4... | collective-permute-start | bytes 786440 | tf_op jit(solution)/shard_map/ppermute | solution.py:17
  31.4 5.8 %collective-permute-start.3 = (bf16[256,512]{1,0:T(8,128)(2,1)S(1)}, bf16[256,512]{1,0:T(8,128)(2,1)S(1)}, u32[]{:S(2)}, u32[]{:S(2)}) collective-permute-start(bf16[256,512]{1,0:T(8,128)(2,1)S(1)} %collective-permute-done.2), channel_id=1, source_target_pairs={{0,64},{64,128},{128,192},{192,256},{256,320},{320,384},{384,448},... | collective-permute-start | bytes 786440 | tf_op jit(solution)/shard_map/ppermute | solution.py:15
  31.4 10.9 %collective-permute-start.6 = (bf16[256,512]{1,0:T(8,128)(2,1)S(1)}, bf16[256,512]{1,0:T(8,128)(2,1)S(1)}, u32[]{:S(2)}, u32[]{:S(2)}) collective-permute-start(bf16[256,512]{1,0:T(8,128)(2,1)S(1)} %collective-permute-done.5), channel_id=1, source_target_pairs={{0,448},{64,0},{128,64},{192,128},{256,192},{320,256},{384,320},{4... | collective-permute-start | bytes 786440 | tf_op jit(solution)/shard_map/ppermute | solution.py:17
  202.3 122.7 %reduce-scatter.2.cloned.1.call-start = ((), (), s32[]{:S(2)}) async-start(), calls=%async_computation.4 | async-start | bytes 2621440 | tf_op jit(solution)/shard_map/reduce_scatter | solution.py:68
Sparse Core Ops, SparseCore 0:
  9.8 96.0 all-gather.5
  107.9 125.7 all-gather.3
  235.8 27.5 all-gather.7
  270.1 54.8 reduce-scatter.1
